TPU v7x, 512 devices: a whole 4x4x16 slice. The times are simulated.
512 devices in a mesh: seg: 16 (over z_hi, x, core), lat: 32 (over z_lo, y).
Axes of the slice: x: 4, y: 4, z: 16 (z_hi: 2, z_lo: 8; z = z_hi * 8 + z_lo), core: 2. Of those that a mesh axis runs over, the one named last changes fastest.
Arguments:
- states: bfloat16 [16, 256, 32, 1024], P('seg', 'lat'), may hold values from -20 to 20
- norm_gain: float32 [1024], replicated, may hold values from 0.1 to 1.9
- w_query: bfloat16 [1024, 512], replicated, may hold values from -1.5 to 1.5
- w_kv: bfloat16 [1024, 1024], replicated, may hold values from -1.5 to 1.5
- reach_rows: int32 [256], P('lat'), may hold values from 1 to 4, as said below
- mem_keep: int32 [16, 32], P('seg', 'lat'), may hold values from 0 to 1, as said below
- d_context: bfloat16 [16, 256, 32, 512], P('seg', 'lat'), may hold values from -6 to 6
Outputs:
- context: bfloat16 [16, 256, 32, 512], P('seg', 'lat')
- grad_states: bfloat16 [16, 256, 32, 1024], P('seg', 'lat')
Inputs may be any that keep to these rules, and one draw needn't show every extreme that they name: `reach_rows`: 4 occurs in every draw. `mem_keep`: 1 where a band of a segment continues the record of its predecessor; among segments 1 to 15 every draw has some 0 and some 1.
All inputs are finite; a program needn't handle non-finite values.
Results may differ from a plain program's by a relative error of at most 0.023.
The roundings to bfloat16 on the way count: a program that leaves them out, or rounds other values in their place, can miss the bound.
Values may be sent and summed in bfloat16 or wider, within the bound.
No kernel may reach another device: no remote copies, remote signals or barrier semaphores. Data moves between devices by JAX's collectives and lax.ppermute only.
A program may use at most 64 MiB of HBM per device.

v0:
```python
import jax
import jax.numpy as jnp
from jax import lax
from jax.sharding import PartitionSpec as P

HEAD_DIM = 64
HALO = 4


NORM_EPS = 1e-06


def passed_along(value, axis, by):
    devices = lax.axis_size(axis)
    pairs = [(i, i + by) for i in range(devices) if 0 <= i + by < devices]
    return lax.ppermute(value, axis, pairs)


def extended(block, sides, width):
    for axis, dim in sides:
        count = lax.axis_size(axis)
        forward = [(i, i + 1) for i in range(count - 1)]
        backward = [(target, source) for source, target in forward]
        low = lax.ppermute(
            lax.slice_in_dim(block, block.shape[dim] - width, None, axis=dim), axis, forward
        )
        high = lax.ppermute(lax.slice_in_dim(block, 0, width, axis=dim), axis, backward)
        block = jnp.concatenate([low, block, high], axis=dim)
    return block


def mix(form, left, right):
    return jnp.einsum(form, left, right, preferred_element_type=jnp.float32)


def dot_back(left, weight):
    return lax.dot_general(
        left, weight, (((1,), (1,)), ((), ())), preferred_element_type=jnp.float32
    )


def attend(queries, window, memory, reach_band, top_ok, bottom_ok, mem_ok, d_ctx):
    row_count, lon_count, inner_width = queries.shape
    key_rows = window.shape[0]
    halo_rows = (key_rows - row_count) // 2
    head_count = inner_width // HEAD_DIM
    tok_count = row_count * lon_count
    near_count = key_rows * lon_count
    query_tok = queries.reshape(tok_count, head_count, HEAD_DIM)
    joined = jnp.concatenate(
        [window.reshape(near_count, 2 * inner_width), memory.reshape(tok_count, 2 * inner_width)], 0
    )
    key_tok = joined[:, :inner_width].reshape(-1, head_count, HEAD_DIM)
    value_tok = joined[:, inner_width:].reshape(-1, head_count, HEAD_DIM)
    query_row = jnp.arange(row_count, dtype=jnp.int32)[:, None]
    key_row = jnp.arange(key_rows, dtype=jnp.int32)[None, :]
    row_gap = key_row - halo_rows - query_row
    inside = (key_row >= halo_rows) | top_ok
    inside = inside & ((key_row < halo_rows + row_count) | bottom_ok)
    usable = (jnp.abs(row_gap) <= reach_band[:, None]) & inside
    near_mask = jnp.broadcast_to(
        usable[:, None, :, None], (row_count, lon_count, key_rows, lon_count)
    ).reshape(tok_count, near_count)
    far_mask = jnp.broadcast_to(mem_ok, (tok_count, tok_count))
    allowed = jnp.concatenate([near_mask, far_mask], 1)
    scores = mix("qhd,khd->hqk", query_tok, key_tok) * HEAD_DIM ** (-0.5)
    scores = jnp.where(allowed[None], scores, -jnp.inf)
    row_max = jnp.max(scores, axis=-1, keepdims=True)
    lifted = jnp.exp(scores - row_max)
    weights = lifted / jnp.sum(lifted, axis=-1, keepdims=True)
    probs = weights.astype(jnp.bfloat16)
    context = mix("hqk,khd->qhd", probs, value_tok).astype(jnp.bfloat16)
    d_out = d_ctx.reshape(tok_count, head_count, HEAD_DIM)
    d_prob = mix("qhd,khd->hqk", d_out, value_tok)
    centre = jnp.sum(weights * d_prob, axis=-1, keepdims=True)
    d_score = (weights * (d_prob - centre) * HEAD_DIM ** (-0.5)).astype(jnp.bfloat16)
    d_query = mix("hqk,khd->qhd", d_score, key_tok).astype(jnp.bfloat16)
    d_key = mix("hqk,qhd->khd", d_score[:, :, :near_count], query_tok).astype(jnp.bfloat16)
    d_value = mix("hqk,qhd->khd", probs[:, :, :near_count], d_out).astype(jnp.bfloat16)
    d_window = jnp.concatenate(
        [d_key.reshape(near_count, inner_width), d_value.reshape(near_count, inner_width)], 1
    )
    return (
        context.reshape(row_count, lon_count, inner_width),
        d_query.reshape(row_count, lon_count, inner_width),
        d_window.reshape(key_rows, lon_count, 2 * inner_width),
    )


def body(states, norm_gain, w_query, w_kv, reach_rows, mem_keep, d_context):
    row_count, lon_count, model_width = (states.shape[1], states.shape[2], states.shape[3])
    inner_width = w_query.shape[1]
    tok_count = row_count * lon_count
    widened = states[0].reshape(tok_count, model_width).astype(jnp.float32)
    inv_rms = lax.rsqrt(jnp.mean(widened * widened, axis=-1, keepdims=True) + NORM_EPS)
    normed = (widened * inv_rms * norm_gain).astype(jnp.bfloat16)
    queries = jnp.dot(normed, w_query, preferred_element_type=jnp.float32).astype(jnp.bfloat16)
    keyval = jnp.dot(normed, w_kv, preferred_element_type=jnp.float32).astype(jnp.bfloat16)
    keyval_rows = keyval.reshape(row_count, lon_count, 2 * inner_width)
    seg_index = lax.axis_index("seg")
    band_index = lax.axis_index("lat")
    band_count = lax.axis_size("lat")
    top_ok = band_index > 0
    bottom_ok = band_index < band_count - 1
    mem_ok = (seg_index >= 1) & (mem_keep[0, 0] == 1)
    memory = passed_along(keyval_rows, "seg", 1)
    window = extended(keyval_rows, (("lat", 0),), HALO)
    context, d_query, d_window = attend(
        queries.reshape(row_count, lon_count, inner_width),
        window,
        memory,
        reach_rows,
        top_ok,
        bottom_ok,
        mem_ok,
        d_context[0],
    )
    d_near = d_window[HALO : HALO + row_count].reshape(tok_count, 2 * inner_width)
    d_normed = dot_back(d_query.reshape(tok_count, inner_width), w_query) + dot_back(d_near, w_kv)
    d_normed = d_normed.reshape(row_count, lon_count, model_width)
    upward = d_window[:HALO]
    downward = d_window[HALO + row_count :]
    middle = jnp.zeros((row_count - 2 * HALO, lon_count, 2 * inner_width), jnp.bfloat16)
    outgoing = jnp.concatenate([upward, middle, downward], 0)
    returned = extended(outgoing, (("lat", 0),), HALO)
    incoming = jnp.concatenate([returned[:HALO], returned[HALO + row_count :]], 0)
    extra = dot_back(incoming.reshape(2 * HALO * lon_count, 2 * inner_width), w_kv)
    extra = extra.reshape(2 * HALO, lon_count, model_width)
    d_normed = jnp.concatenate(
        [
            d_normed[:HALO] + extra[:HALO],
            d_normed[HALO : row_count - HALO],
            d_normed[row_count - HALO :] + extra[HALO:],
        ],
        0,
    )
    d_normed = d_normed.reshape(tok_count, model_width)
    scaled = d_normed * norm_gain
    grad = inv_rms * scaled - widened * inv_rms**3 * jnp.mean(
        scaled * widened, axis=-1, keepdims=True
    )
    grad_states = grad.astype(jnp.bfloat16).reshape(1, row_count, lon_count, model_width)
    return (context.reshape(1, row_count, lon_count, inner_width), grad_states)


def solution(mesh):
    return jax.shard_map(
        body,
        mesh=mesh,
        in_specs=(
            P("seg", "lat", None, None),
            P(),
            P(),
            P(),
            P("lat"),
            P("seg", "lat"),
            P("seg", "lat", None, None),
        ),
        out_specs=(P("seg", "lat", None, None), P("seg", "lat", None, None)),
        check_vma=False,
    )
```

profile of v0, /device:TPU:280, one launch (start us, length us, event | category | flops | bytes accessed | tf_op | source)
XLA Modules:
  0.0 109.0 jit_solution(12729640752442110510)
XLA Ops:
  0.7 1.4 %multiply_reduce_fusion = f32[8,32]{1,0:T(8,128)S(1)} fusion(bf16[1,8,32,1024]{3,2,1,0:T(8,128)(2,1)} %param.7), kind=kLoop, calls=%fused_computation.44 | loop fusion | flops 786176 | bytes 525312 | tf_op jit(solution)/shard_map/reduce_sum | solution.py:95
  4.3 1.5 %convolution_convert_fusion = bf16[256,1024]{1,0:T(8,128)(2,1)} fusion(bf16[256,1024]{1,0:T(8,128)(2,1)S(1)} %fusion.27, bf16[1024,1024]{1,0:T(8,128)(2,1)S(1)} %copy-done), kind=kOutput, calls=%fused_computation.24 | convolution fusion | flops 537133056 | bytes 3145728 | tf_op jit(solution)/shard_map/dot_general | solution.py:98
  5.8 1.9 %fusion.42 = (bf16[128,1024]{1,0:T(8,128)(2,1)}, bf16[128,1024]{1,0:T(8,128)(2,1)}) fusion(bf16[256,1024]{1,0:T(8,128)(2,1)} %convolution_convert_fusion), kind=kLoop, calls=%fused_computation.67 | loop fusion | bytes 1048576 | tf_op jit(solution)/shard_map/slice | solution.py:25
  7.6 2.6 %collective-permute-start = (bf16[4,32,1024]{2,1,0:T(8,128)(2,1)}, bf16[4,32,1024]{2,1,0:T(8,128)(2,1)}, u32[]{:S(2)}, u32[]{:S(2)}) collective-permute-start(bf16[4,32,1024]{2,1,0:T(8,128)(2,1)} %bitcast.1), channel_id=1, source_target_pairs={{0,1},{1,2},{2,3},{3,4},{4,5},{5,6},{6,7},{7,8},{8,9},{9,10},{10,1... | collective-permute-start | bytes 786440 | tf_op jit(solution)/shard_map/ppermute | solution.py:24
  10.2 3.3 %collective-permute-start.1 = (bf16[4,32,1024]{2,1,0:T(8,128)(2,1)}, bf16[4,32,1024]{2,1,0:T(8,128)(2,1)}, u32[]{:S(2)}, u32[]{:S(2)}) collective-permute-start(bf16[4,32,1024]{2,1,0:T(8,128)(2,1)} %bitcast.3), channel_id=1, source_target_pairs={{1,0},{2,1},{3,2},{4,3},{5,4},{6,5},{7,6},{8,7},{9,8},{10,9},{11,1... | collective-permute-start | bytes 786440 | tf_op jit(solution)/shard_map/ppermute | solution.py:27
  13.5 1.9 %collective-permute-start.2 = (bf16[8,32,1024]{2,1,0:T(8,128)(2,1)}, bf16[8,32,1024]{2,1,0:T(8,128)(2,1)}, u32[]{:S(2)}, u32[]{:S(2)}) collective-permute-start(bf16[8,32,1024]{2,1,0:T(8,128)(2,1)} %bitcast.2), channel_id=1, source_target_pairs={{0,32},{32,64},{64,96},{96,128},{128,160},{160,192},{192,224},{224... | collective-permute-start | bytes 1572872 | tf_op jit(solution)/shard_map/ppermute | solution.py:16
  16.5 2.1 %reshape.226 = pred[256,512]{1,0:T(8,128)(4,1)S(1)} reshape(pred[8,32,16,32]{3,2,1,0:T(8,128)(4,1)} %broadcast_in_dim.10) | data formatting | bytes 262144 | tf_op jit(solution)/shard_map/reshape | solution.py:63
  19.3 1.5 %convolution_convert_fusion.3 = bf16[256,512]{1,0:T(8,128)(2,1)S(1)} fusion(bf16[256,1024]{1,0:T(8,128)(2,1)} %copy-done.8, bf16[1024,512]{1,0:T(8,128)(2,1)S(1)} %copy-done.4), kind=kOutput, calls=%fused_computation.27 | convolution fusion | flops 268566528 | bytes 1835008 | tf_op jit(solution)/shard_map/dot_general | solution.py:97
  23.9 2.3 %pad_maximum_fusion = bf16[16,32,1024]{2,1,0:T(8,128)(2,1)} fusion(bf16[4,32,1024]{2,1,0:T(8,128)(2,1)} %collective-permute-done.1, bf16[8,32,1024]{2,1,0:T(8,128)(2,1)} %bitcast.2, bf16[4,32,1024]{2,1,0:T(8,128)(2,1)} %collective-permute-done), kind=kLoop, calls=%fused_computation.33 | loop fusion | flops 1048576 | bytes 2097152 | tf_op jit(solution)/shard_map/concatenate | solution.py:28
  26.2 1.5 %copy.17 = bf16[512,1024]{0,1:T(8,128)(2,1)S(1)} copy(bf16[512,1024]{1,0:T(8,128)(2,1)} %bitcast.80) | data formatting | bytes 2097152 | tf_op jit(solution)/shard_map/reshape | solution.py:51
  27.7 7.7 %collective-permute-done.2 = bf16[8,32,1024]{2,1,0:T(8,128)(2,1)} collective-permute-done((bf16[8,32,1024]{2,1,0:T(8,128)(2,1)}, bf16[8,32,1024]{2,1,0:T(8,128)(2,1)}, u32[]{:S(2)}, u32[]{:S(2)}) %collective-permute-start.2) | collective-permute-done | bytes 524320 | tf_op jit(solution)/shard_map/ppermute | solution.py:16
  35.4 2.0 %copy.18 = bf16[256,1024]{0,1:T(8,128)(2,1)} copy(bf16[256,1024]{1,0:T(8,128)(2,1)} %bitcast.5) | data formatting | bytes 1048576 | tf_op jit(solution)/shard_map/reshape | solution.py:51
  37.4 2.3 %pad_maximum_fusion.1 = (bf16[768,512]{0,1:T(8,128)(2,1)}, bf16[768,512]{0,1:T(8,128)(2,1)}) fusion(bf16[256,1024]{0,1:T(8,128)(2,1)} %copy.18, bf16[512,1024]{0,1:T(8,128)(2,1)S(1)} %copy.17), kind=kLoop, calls=%fused_computation.46 | loop fusion | flops 3145728 | bytes 3145728 | tf_op jit(solution)/shard_map/concatenate | solution.py:50
  39.7 6.2 %fusion.43 = (f32[8,256]{1,0:T(8,128)S(1)}, f32[8,256,768]{2,1,0:T(8,128)}) fusion(pred[256,768]{1,0:T(8,128)(4,1)} %concatenate.31, bf16[256,8,64]{0,2,1:T(8,128)(2,1)} %bitcast.89, bf16[768,8,64]{0,2,1:T(8,128)(2,1)} %bitcast.83), kind=kOutput, calls=%fused_computation.68 | convolution fusion | flops 207618816 | bytes 7544832 | tf_op jit(solution)/shard_map/sub | solution.py:69
  46.0 10.2 %fusion.4 = bf16[8,256,768]{2,1,0:T(8,128)(2,1)} fusion(bf16[768,8,64]{0,2,1:T(8,128)(2,1)S(1)} %bitcast.81, bf16[256,8,64]{0,2,1:T(8,128)(2,1)S(1)} %copy.21, f32[8,256,768]{2,1,0:T(8,128)} %get-tuple-element.15, f32[8,256]{1,0:T(8,128)S(1)} %get-tuple-element.14), kind=kOutput, calls=%fused_computation.6 | convolution fusion | flops 413666048 | bytes 10493952 | tf_op jit(solution)/shard_map/sub | solution.py:76
  56.1 4.0 %convolution_convert_fusion.1 = bf16[8,64,256]{2,1,0:T(8,128)(2,1)} fusion(bf16[768,8,64]{0,2,1:T(8,128)(2,1)} %bitcast.84, bf16[8,256,768]{2,1,0:T(8,128)(2,1)} %fusion.4), kind=kOutput, calls=%fused_computation.25 | convolution fusion | flops 201457664 | bytes 4194304 | tf_op jit(solution)/shard_map/hqk,khd->qhd/dot_general | solution.py:33
  60.7 5.0 %fusion.41 = bf16[8,256,768]{2,1,0:T(8,128)(2,1)} fusion(f32[8,256,768]{2,1,0:T(8,128)} %get-tuple-element.15, f32[8,256]{1,0:T(8,128)S(1)} %get-tuple-element.14), kind=kLoop, calls=%fused_computation.66 | loop fusion | flops 3145728 | bytes 9445376 | tf_op jit(solution)/shard_map/convert_element_type | solution.py:71
  65.9 2.9 %fusion.17 = bf16[8,512,64]{1,2,0:T(8,128)(2,1)} fusion(bf16[256,8,64]{0,2,1:T(8,128)(2,1)S(1)} %copy.21, bf16[8,256,768]{2,1,0:T(8,128)(2,1)} %fusion.41), kind=kOutput, calls=%fused_computation.23 | convolution fusion | flops 134479872 | bytes 2883584 | tf_op jit(solution)/shard_map/hqk,qhd->khd/dot_general | solution.py:33
  70.0 1.7 %fusion.34 = f32[256,1024]{1,0:T(8,128)} fusion(bf16[1024,1024]{1,0:T(8,128)(2,1)S(1)} %copy-done, bf16[512,512]{1,0:T(8,128)(2,1)S(1)} %copy.24, bf16[512,512]{1,0:T(8,128)(2,1)S(1)} %copy.25), kind=kOutput, calls=%fused_computation.50 | convolution fusion | flops 537919488 | bytes 4194304 | tf_op jit(solution)/shard_map/dot_general | solution.py:37
  73.7 21.2 %collective-permute-start.3 = (bf16[4,32,1024]{2,1,0:T(8,128)(2,1)}, bf16[4,32,1024]{2,1,0:T(8,128)(2,1)}, u32[]{:S(2)}, u32[]{:S(2)}) collective-permute-start(bf16[4,32,1024]{2,1,0:T(8,128)(2,1)} %bitcast.18), channel_id=1, source_target_pairs={{0,1},{1,2},{2,3},{3,4},{4,5},{5,6},{6,7},{7,8},{8,9},{9,10},{10,1... | collective-permute-start | bytes 786440 | tf_op jit(solution)/shard_map/ppermute | solution.py:24
  94.9 1.9 %collective-permute-start.4 = (bf16[4,32,1024]{2,1,0:T(8,128)(2,1)}, bf16[4,32,1024]{2,1,0:T(8,128)(2,1)}, u32[]{:S(2)}, u32[]{:S(2)}) collective-permute-start(bf16[4,32,1024]{2,1,0:T(8,128)(2,1)} %bitcast.19), channel_id=1, source_target_pairs={{1,0},{2,1},{3,2},{4,3},{5,4},{6,5},{7,6},{8,7},{9,8},{10,9},{11,1... | collective-permute-start | bytes 786440 | tf_op jit(solution)/shard_map/ppermute | solution.py:27
  97.9 2.1 %reshape_reshape.10 = bf16[1,8,32,512]{3,2,1,0:T(8,128)(2,1)} reshape(bf16[256,8,64]{2,1,0:T(8,128)(2,1)} %copy.20) | data formatting | bytes 524288 | tf_op jit(solution)/shard_map/reshape;reshape | solution.py:143
  100.0 1.8 %convolution_add_fusion = f32[256,1024]{1,0:T(8,128)S(1)} fusion(f32[256,1024]{1,0:T(8,128)} %fusion.34, bf16[256,512]{0,1:T(8,128)(2,1)} %bitcast.88, bf16[1024,512]{1,0:T(8,128)(2,1)S(1)} %copy-done.5), kind=kOutput, calls=%fused_computation.21 | convolution fusion | flops 268697600 | bytes 3407872 | tf_op jit(solution)/shard_map/dot_general | solution.py:37
  101.8 3.8 %collective-permute-done.4 = bf16[4,32,1024]{2,1,0:T(8,128)(2,1)} collective-permute-done((bf16[4,32,1024]{2,1,0:T(8,128)(2,1)}, bf16[4,32,1024]{2,1,0:T(8,128)(2,1)}, u32[]{:S(2)}, u32[]{:S(2)}) %collective-permute-start.4) | collective-permute-done | bytes 262176 | tf_op jit(solution)/shard_map/ppermute | solution.py:27
  (50 shorter events, 14.8 us)
Async XLA Ops:
  0.6 3.6 %copy-start = (bf16[1024,1024]{1,0:T(8,128)(2,1)S(1)}, bf16[1024,1024]{1,0:T(8,128)(2,1)}, u32[]{:S(2)}) copy-start(bf16[1024,1024]{1,0:T(8,128)(2,1)} %param.10) | copy-start | bytes 6291460
  0.6 14.8 %copy-start.11 = (s32[8]{0:T(128)S(1)}, s32[8]{0:T(128)}, u32[]{:S(2)}) copy-start(s32[8]{0:T(128)} %param.11) | copy-start | bytes 100
  2.1 17.1 %copy-start.4 = (bf16[1024,512]{1,0:T(8,128)(2,1)S(1)}, bf16[1024,512]{1,0:T(8,128)(2,1)}, u32[]{:S(2)}) copy-start(bf16[1024,512]{1,0:T(8,128)(2,1)} %param.9) | copy-start | bytes 3145732
  3.4 0.8 copy-start.8
  7.6 16.3 %collective-permute-start = (bf16[4,32,1024]{2,1,0:T(8,128)(2,1)}, bf16[4,32,1024]{2,1,0:T(8,128)(2,1)}, u32[]{:S(2)}, u32[]{:S(2)}) collective-permute-start(bf16[4,32,1024]{2,1,0:T(8,128)(2,1)} %bitcast.1), channel_id=1, source_target_pairs={{0,1},{1,2},{2,3},{3,4},{4,5},{5,6},{6,7},{7,8},{8,9},{9,10},{10,1... | collective-permute-start | bytes 786440 | tf_op jit(solution)/shard_map/ppermute | solution.py:24
  10.2 13.7 %collective-permute-start.1 = (bf16[4,32,1024]{2,1,0:T(8,128)(2,1)}, bf16[4,32,1024]{2,1,0:T(8,128)(2,1)}, u32[]{:S(2)}, u32[]{:S(2)}) collective-permute-start(bf16[4,32,1024]{2,1,0:T(8,128)(2,1)} %bitcast.3), channel_id=1, source_target_pairs={{1,0},{2,1},{3,2},{4,3},{5,4},{6,5},{7,6},{8,7},{9,8},{10,9},{11,1... | collective-permute-start | bytes 786440 | tf_op jit(solution)/shard_map/ppermute | solution.py:27
  13.5 21.9 %collective-permute-start.2 = (bf16[8,32,1024]{2,1,0:T(8,128)(2,1)}, bf16[8,32,1024]{2,1,0:T(8,128)(2,1)}, u32[]{:S(2)}, u32[]{:S(2)}) collective-permute-start(bf16[8,32,1024]{2,1,0:T(8,128)(2,1)} %bitcast.2), channel_id=1, source_target_pairs={{0,32},{32,64},{64,96},{96,128},{128,160},{160,192},{192,224},{224... | collective-permute-start | bytes 1572872 | tf_op jit(solution)/shard_map/ppermute | solution.py:16
  39.7 6.2 %copy-start.6 = (bf16[768,512]{0,1:T(8,128)(2,1)S(1)}, bf16[768,512]{0,1:T(8,128)(2,1)}, u32[]{:S(2)}) copy-start(bf16[768,512]{0,1:T(8,128)(2,1)} %get-tuple-element.7) | copy-start | bytes 2359300
  56.1 4.1 %copy-start.2 = (bf16[8,256,768]{2,1,0:T(8,128)(2,1)S(1)}, bf16[8,256,768]{2,1,0:T(8,128)(2,1)}, u32[]{:S(2)}) copy-start(bf16[8,256,768]{2,1,0:T(8,128)(2,1)} %fusion.4) | copy-start | bytes 9437188
  56.1 4.1 %copy-start.9 = (bf16[256,512]{0,1:T(8,128)(2,1)S(1)}, bf16[256,512]{0,1:T(8,128)(2,1)}, u32[]{:S(2)}) copy-start(bf16[256,512]{0,1:T(8,128)(2,1)} %copy.19) | copy-start | bytes 786436
  70.0 2.6 %copy-start.1 = (bf16[8,256,768]{2,1,0:T(8,128)(2,1)S(1)}, bf16[8,256,768]{2,1,0:T(8,128)(2,1)}, u32[]{:S(2)}) copy-start(bf16[8,256,768]{2,1,0:T(8,128)(2,1)} %fusion.41) | copy-start | bytes 9437188
  70.0 2.6 %copy-start.7 = (bf16[768,512]{0,1:T(8,128)(2,1)S(1)}, bf16[768,512]{0,1:T(8,128)(2,1)}, u32[]{:S(2)}) copy-start(bf16[768,512]{0,1:T(8,128)(2,1)} %get-tuple-element.7) | copy-start | bytes 2359300
  72.6 27.4 %copy-start.5 = (bf16[1024,512]{1,0:T(8,128)(2,1)S(1)}, bf16[1024,512]{1,0:T(8,128)(2,1)}, u32[]{:S(2)}) copy-start(bf16[1024,512]{1,0:T(8,128)(2,1)} %param.9) | copy-start | bytes 3145732
  73.7 28.2 %collective-permute-start.3 = (bf16[4,32,1024]{2,1,0:T(8,128)(2,1)}, bf16[4,32,1024]{2,1,0:T(8,128)(2,1)}, u32[]{:S(2)}, u32[]{:S(2)}) collective-permute-start(bf16[4,32,1024]{2,1,0:T(8,128)(2,1)} %bitcast.18), channel_id=1, source_target_pairs={{0,1},{1,2},{2,3},{3,4},{4,5},{5,6},{6,7},{7,8},{8,9},{9,10},{10,1... | collective-permute-start | bytes 786440 | tf_op jit(solution)/shard_map/ppermute | solution.py:24
  94.9 10.7 %collective-permute-start.4 = (bf16[4,32,1024]{2,1,0:T(8,128)(2,1)}, bf16[4,32,1024]{2,1,0:T(8,128)(2,1)}, u32[]{:S(2)}, u32[]{:S(2)}) collective-permute-start(bf16[4,32,1024]{2,1,0:T(8,128)(2,1)} %bitcast.19), channel_id=1, source_target_pairs={{1,0},{2,1},{3,2},{4,3},{5,4},{6,5},{7,6},{8,7},{9,8},{10,9},{11,1... | collective-permute-start | bytes 786440 | tf_op jit(solution)/shard_map/ppermute | solution.py:27
  106.7 1.0 copy-start.3
  106.7 1.0 copy-start.10
where the time goes:
time: 110 us; the launch traced here: 109 us
  matrix products  32.1 us (29%)
  starting transfers between devices  30.9 us (28%)
  local copies, waits for them, and re-layouts  17.3 us (16%)
  other arithmetic  15.7 us (14%)
  waiting for transfers between devices  11.5 us (10%)
  between operations  1.56 us (1%)
    ppermute x2, starting transfers between devices, extended(): lax.ppermute(lax.slice_in_dim(block, block.shape[dim] - width, None, axis...  23.8 us
    sub x1, matrix products, attend(): d_prob - centre  10.2 us
    dot_general x4, matrix products, mix(): return jnp.einsum(form, left, right, preferred_element_type=jnp.float32)  8.45 us
    ppermute x1, waiting for transfers between devices, passed_along(): return lax.ppermute(value, axis, pairs)  7.72 us
    sub x1, matrix products, attend(): lifted = jnp.exp(scores - row_max)  6.23 us
    ppermute x2, starting transfers between devices, extended(): lax.ppermute(lax.slice_in_dim(block, 0, width, axis=dim), axis, backward)  5.18 us
    convert_element_type x1, other arithmetic, attend(): probs = weights.astype(jnp.bfloat16)  4.96 us
    dot_general x3, matrix products, dot_back(): lax.dot_general(left, weight, (((1,), (1,)), ((), ())), preferred_element...  4.25 us
  transfers between devices with their start and end apart: 5, of which 2 were waited for; matrix products, arithmetic and copies ran while one was open for 15% of the time, Pallas kernels for 0%

commit v1 on v0

v1 whole, which is shorter than its diff:
```python
import jax
import jax.numpy as jnp
from jax import lax
from jax.experimental import pallas as pl
from jax.experimental.pallas import tpu as pltpu
from jax.sharding import PartitionSpec as P

HEAD_DIM = 64
HALO = 4
NORM_EPS = 1e-06
NEG = -1e30
BF = jnp.bfloat16
F32 = jnp.float32
VMEM_LIMIT = 40 * 1024 * 1024


def dot(a, b):
    return lax.dot_general(a, b, (((1,), (0,)), ((), ())), preferred_element_type=F32)


def dot_nt(a, b):
    return lax.dot_general(a, b, (((1,), (1,)), ((), ())), preferred_element_type=F32)


def inv_rms_of(wide):
    return lax.rsqrt(jnp.mean(wide * wide, axis=-1, keepdims=True) + NORM_EPS)


def project_kernel(states_ref, gain_ref, wq_ref, wkv_ref, q_ref, kv_ref):
    wide = states_ref[...].astype(F32)
    normed = (wide * inv_rms_of(wide) * gain_ref[...]).astype(BF)
    kv_ref[...] = dot(normed, wkv_ref[...]).astype(BF)
    q_ref[...] = dot(normed, wq_ref[...]).astype(BF)


def project(states, gain, w_query, w_kv):
    toks, width = states.shape
    inner = w_query.shape[1]
    return pl.pallas_call(
        project_kernel,
        out_shape=(
            jax.ShapeDtypeStruct((toks, inner), BF),
            jax.ShapeDtypeStruct((toks, 2 * inner), BF),
        ),
        compiler_params=pltpu.CompilerParams(vmem_limit_bytes=VMEM_LIMIT),
        cost_estimate=pl.CostEstimate(
            flops=6 * toks * width * inner, bytes_accessed=6 * width * inner, transcendentals=0
        ),
        name="project",
    )(states, gain, w_query, w_kv)


def bias_of(reach_ref, keep_ref, toks, lon):
    row = lax.broadcasted_iota(jnp.int32, (128, toks), 0)
    own = lax.broadcasted_iota(jnp.int32, (128, toks), 1) // lon
    reach = jnp.zeros((128, toks), jnp.int32)
    for i in range(2 * HALO):
        reach = jnp.where(own == i, reach_ref[i], reach)
    seg, band = lax.axis_index("seg"), lax.axis_index("lat")
    low = jnp.where(band > 0, 0, HALO)
    high = jnp.where(band < lax.axis_size("lat") - 1, 4 * HALO, 3 * HALO)
    mem_bias = jnp.where((seg >= 1) & (keep_ref[0] == 1), 0.0, NEG)
    usable = (jnp.abs(row - HALO - own) <= reach) & (row >= low) & (row < high)
    bias = jnp.where(usable, 0.0, NEG)
    bias = jnp.where(row == 4 * HALO, mem_bias, bias)
    return jnp.where(row > 4 * HALO, 0.0, bias).astype(BF)


def marked(keys, first, lon):
    count = keys.shape[0]
    col = lax.broadcasted_iota(jnp.int32, (count, 128), 1)
    if first == 4 * HALO:
        hot = col == first
    else:
        hot = col == first + lax.broadcasted_iota(jnp.int32, (count, 128), 0) // lon
    return jnp.concatenate([keys, jnp.where(hot, 1.0, 0.0).astype(BF)], axis=1)


def head_rows(h):
    return slice(h * HEAD_DIM, (h + 1) * HEAD_DIM)


def only_head(value, h):
    lane = lax.broadcasted_iota(jnp.int32, value.shape, 1)
    mine = (lane >= h * HEAD_DIM) & (lane < (h + 1) * HEAD_DIM)
    return jnp.where(mine, value, jnp.zeros_like(value))


def padded_t(value_t, h, below=()):
    zeros = jnp.zeros((HEAD_DIM, value_t.shape[1]), value_t.dtype)
    pieces = [zeros, zeros]
    pieces[h] = value_t[head_rows(h)]
    return jnp.concatenate(pieces + list(below), axis=0)


def halves(left_up, left_dn, right):
    half = right.shape[1] // 2
    return jnp.concatenate([dot(left_up, right[:, :half]), dot(left_dn, right[:, half:])], axis=1)


def window_kernel(
    reach_ref, keep_ref,
    q_ref, k_ref, v_ref, ku_ref, vu_ref, kd_ref, vd_ref, do_ref,
    ctx_ref, stats_ref, e_ref, d_ref,
):
    toks = q_ref.shape[0]
    half = toks // 2
    lon = half // HALO
    bias = bias_of(reach_ref, keep_ref, toks, lon)
    kx_own = marked(k_ref[...], HALO, lon)
    kx_up, kx_dn = marked(ku_ref[...], 0, lon), marked(kd_ref[...], 3 * HALO, lon)
    v_up, v_dn = vu_ref[...], vd_ref[...]
    q_t, do_t = (q_ref[...] * jnp.asarray(HEAD_DIM ** (-0.5), BF)).T, do_ref[...].T
    vt_own, vt_up, vt_dn = v_ref[...].T, v_up.T, v_dn.T
    for h in range(2):
        rows = head_rows(h)
        qt_h = padded_t(q_t, h, (bias,))
        s_own, s_halo = dot(kx_own, qt_h), halves(kx_up, kx_dn, qt_h)
        d_ref[h] = halves(v_up, v_dn, padded_t(do_t, h))
        top = jnp.maximum(jnp.max(s_own, axis=0, keepdims=True), jnp.max(s_halo, axis=0, keepdims=True))
        e_own, e_halo = jnp.exp(s_own - top), jnp.exp(s_halo - top)
        e_ref[h] = e_halo
        total = jnp.sum(e_own, axis=0, keepdims=True) + jnp.sum(e_halo, axis=0, keepdims=True)
        stats_ref[0, 2 * h : 2 * h + 2, :] = jnp.concatenate([top, total], axis=0)
        ctx_ref[rows] = dot(vt_own[rows], e_own.astype(BF)) + halves(vt_up[rows], vt_dn[rows], e_halo.astype(BF))


def outer_kernel(
    keep_ref,
    q_ref, km_ref, vm_ref, do_ref, part_ref, window_ref, e_ref, d_ref,
    ctx_ref, stats_ref, g_ref, dup_ref, ddn_ref,
):
    toks = q_ref.shape[0]
    half = toks // 2
    mem_bias = jnp.where((lax.axis_index("seg") >= 1) & (keep_ref[0] == 1), 0.0, NEG)
    bias = jnp.where(lax.broadcasted_iota(jnp.int32, (128, toks), 0) == 4 * HALO, mem_bias, 0.0).astype(BF)
    kx_mem = marked(km_ref[...], 4 * HALO, half // HALO)
    q = q_ref[...] * jnp.asarray(HEAD_DIM ** (-0.5), BF)
    d_out = do_ref[...]
    q_t, do_t, vt_mem = q.T, d_out.T, vm_ref[...].T
    sums = None
    ctx_parts = []
    for h in range(2):
        rows = head_rows(h)
        s_mem = dot(kx_mem, padded_t(q_t, h, (bias,)))
        before, part = window_ref[0, 2 * h : 2 * h + 1, :], window_ref[0, 2 * h + 1 : 2 * h + 2, :]
        top = jnp.maximum(jnp.max(s_mem, axis=0, keepdims=True), before)
        e_mem = jnp.exp(s_mem - top)
        fade = jnp.exp(before - top)
        inv = 1.0 / (part * fade + jnp.sum(e_mem, axis=0, keepdims=True))
        fade = fade * inv
        ctx_t = part_ref[rows] * fade + dot(vt_mem[rows], (e_mem * inv).astype(BF))
        centre = jnp.sum(ctx_t * do_t[rows].astype(F32), axis=0, keepdims=True)
        w_halo = e_ref[h] * fade
        p_halo = w_halo.astype(BF)
        g_halo = (w_halo * (d_ref[h] - centre)).astype(BF)
        stats_ref[0, 3 * h : 3 * h + 3, :] = jnp.concatenate([top, inv, centre], axis=0)
        g_ref[h] = g_halo
        ctx_parts.append(ctx_t)
        q_h, do_h = only_head(q, h), only_head(d_out, h)
        terms = (
            dot(g_halo[:, :half], q_h[:half]), dot(p_halo[:, :half], do_h[:half]),
            dot(g_halo[:, half:], q_h[half:]), dot(p_halo[:, half:], do_h[half:]),
        )
        sums = terms if sums is None else tuple(x + y for x, y in zip(sums, terms))
    dup_ref[0] = sums[0].astype(BF)
    dup_ref[1] = sums[1].astype(BF)
    ddn_ref[0] = sums[2].astype(BF)
    ddn_ref[1] = sums[3].astype(BF)
    ctx_ref[...] = jnp.concatenate(ctx_parts, axis=0).T.astype(BF)


def inner_kernel(
    reach_ref, keep_ref,
    q_ref, k_ref, v_ref, ku_ref, kd_ref, km_ref, vm_ref, do_ref, stats_ref, g_ref,
    dq_ref, dnear_ref,
):
    toks = q_ref.shape[0]
    lon = toks // (2 * HALO)
    scale = HEAD_DIM ** (-0.5)
    bias = bias_of(reach_ref, keep_ref, toks, lon)
    k_own, k_mem, v_own, v_mem = k_ref[...], km_ref[...], v_ref[...], vm_ref[...]
    kx_own, kx_mem = marked(k_own, HALO, lon), marked(k_mem, 4 * HALO, lon)
    q = q_ref[...] * jnp.asarray(scale, BF)
    d_out = do_ref[...]
    q_t, do_t = q.T, d_out.T
    kt_own, kt_up, kt_dn, kt_mem = k_own.T, ku_ref[...].T, kd_ref[...].T, k_mem.T
    sums = None
    dq_parts = []
    for h in range(2):
        rows = head_rows(h)
        qt_h = padded_t(q_t, h, (bias,))
        dot_h = padded_t(do_t, h)
        top, inv, centre = (stats_ref[0, 3 * h + i : 3 * h + i + 1, :] for i in range(3))
        w_own = jnp.exp(dot(kx_own, qt_h) - top) * inv
        w_mem = jnp.exp(dot(kx_mem, qt_h) - top) * inv
        g_own = (w_own * (dot(v_own, dot_h) - centre)).astype(BF)
        g_mem = (w_mem * (dot(v_mem, dot_h) - centre)).astype(BF)
        dq_parts.append(
            (dot(kt_own[rows], g_own) + dot(kt_mem[rows], g_mem) + halves(kt_up[rows], kt_dn[rows], g_ref[h]))
            * scale
        )
        terms = dot(g_own, only_head(q, h)), dot(w_own.astype(BF), only_head(d_out, h))
        sums = terms if sums is None else tuple(x + y for x, y in zip(sums, terms))
    dq_ref[...] = jnp.concatenate(dq_parts, axis=0).T.astype(BF)
    dnear_ref[0] = sums[0].astype(BF)
    dnear_ref[1] = sums[1].astype(BF)


def cols(count, shift):
    return pl.BlockSpec((count, 128), lambda i, *_: (0, i + shift))


def lead(lead_count, count, width):
    if width == 128:
        return pl.BlockSpec((lead_count, count, width), lambda i, *_: (0, 0, i))
    return pl.BlockSpec((lead_count, count, width), lambda i, *_: (i, 0, 0))


def attend_window(reach, keep, queries, keyval, halo, d_ctx):
    toks, inner = queries.shape
    half = toks // 2
    pairs = inner // 128
    up = lambda shift: pl.BlockSpec((half, 128), lambda i, *_: (0, i + shift))
    down = lambda shift: pl.BlockSpec((half, 128), lambda i, *_: (1, i + shift))
    return pl.pallas_call(
        window_kernel,
        grid_spec=pltpu.PrefetchScalarGridSpec(
            num_scalar_prefetch=2,
            grid=(pairs,),
            in_specs=[
                cols(toks, 0), cols(toks, 0), cols(toks, pairs),
                up(0), up(pairs), down(0), down(pairs), cols(toks, 0),
            ],
            out_specs=[
                pl.BlockSpec((128, toks), lambda i, *_: (i, 0)),
                lead(1, 8, toks), lead(2, half, toks), lead(2, half, toks),
            ],
        ),
        out_shape=(
            jax.ShapeDtypeStruct((inner, toks), F32),
            jax.ShapeDtypeStruct((pairs, 8, toks), F32),
            jax.ShapeDtypeStruct((2 * pairs, half, toks), F32),
            jax.ShapeDtypeStruct((2 * pairs, half, toks), F32),
        ),
        compiler_params=pltpu.CompilerParams(vmem_limit_bytes=VMEM_LIMIT),
        cost_estimate=pl.CostEstimate(
            flops=24 * toks * toks * inner, bytes_accessed=4 * toks * inner * 10, transcendentals=toks * toks * 16
        ),
        name="attend_window",
    )(reach, keep, queries, keyval, keyval, halo, halo, halo, halo, d_ctx)


def attend_outer(keep, queries, memory, d_ctx, part, window, e_halo, d_halo):
    toks, inner = queries.shape
    half = toks // 2
    pairs = inner // 128
    return pl.pallas_call(
        outer_kernel,
        grid_spec=pltpu.PrefetchScalarGridSpec(
            num_scalar_prefetch=1,
            grid=(pairs,),
            in_specs=[
                cols(toks, 0), cols(toks, 0), cols(toks, pairs), cols(toks, 0),
                pl.BlockSpec((128, toks), lambda i, *_: (i, 0)),
                lead(1, 8, toks), lead(2, half, toks), lead(2, half, toks),
            ],
            out_specs=[
                cols(toks, 0), lead(1, 8, toks), lead(2, half, toks), lead(2, half, 128), lead(2, half, 128),
            ],
        ),
        out_shape=(
            jax.ShapeDtypeStruct((toks, inner), BF),
            jax.ShapeDtypeStruct((pairs, 8, toks), F32),
            jax.ShapeDtypeStruct((2 * pairs, half, toks), BF),
            jax.ShapeDtypeStruct((2, half, inner), BF),
            jax.ShapeDtypeStruct((2, half, inner), BF),
        ),
        compiler_params=pltpu.CompilerParams(vmem_limit_bytes=VMEM_LIMIT),
        cost_estimate=pl.CostEstimate(
            flops=12 * toks * toks * inner, bytes_accessed=4 * toks * inner * 10, transcendentals=toks * toks * 8
        ),
        name="attend_outer",
    )(keep, queries, memory, memory, d_ctx, part, window, e_halo, d_halo)


def attend_inner(reach, keep, queries, keyval, halo, memory, d_ctx, stats, g_halo):
    toks, inner = queries.shape
    half = toks // 2
    pairs = inner // 128
    up = pl.BlockSpec((half, 128), lambda i, *_: (0, i))
    down = pl.BlockSpec((half, 128), lambda i, *_: (1, i))
    return pl.pallas_call(
        inner_kernel,
        grid_spec=pltpu.PrefetchScalarGridSpec(
            num_scalar_prefetch=2,
            grid=(pairs,),
            in_specs=[
                cols(toks, 0), cols(toks, 0), cols(toks, pairs), up, down,
                cols(toks, 0), cols(toks, pairs), cols(toks, 0), lead(1, 8, toks), lead(2, half, toks),
            ],
            out_specs=[cols(toks, 0), lead(2, toks, 128)],
        ),
        out_shape=(
            jax.ShapeDtypeStruct((toks, inner), BF),
            jax.ShapeDtypeStruct((2, toks, inner), BF),
        ),
        compiler_params=pltpu.CompilerParams(vmem_limit_bytes=VMEM_LIMIT),
        cost_estimate=pl.CostEstimate(
            flops=24 * toks * toks * inner, bytes_accessed=4 * toks * inner * 10, transcendentals=toks * toks * 16
        ),
        name="attend_inner",
    )(reach, keep, queries, keyval, keyval, halo, halo, memory, memory, d_ctx, stats, g_halo)


def main_back_kernel(dq_ref, dnear_ref, wq_ref, wkv_ref, out_ref):
    inner = dq_ref.shape[1]
    out_ref[...] = (
        dot_nt(dq_ref[...], wq_ref[...])
        + dot_nt(dnear_ref[0], wkv_ref[:, :inner])
        + dot_nt(dnear_ref[1], wkv_ref[:, inner:])
    )


def main_back(d_query, d_near, w_query, w_kv):
    toks, inner = d_query.shape
    width = w_query.shape[0]
    return pl.pallas_call(
        main_back_kernel,
        out_shape=jax.ShapeDtypeStruct((toks, width), F32),
        compiler_params=pltpu.CompilerParams(vmem_limit_bytes=VMEM_LIMIT),
        cost_estimate=pl.CostEstimate(
            flops=6 * toks * width * inner, bytes_accessed=6 * width * inner, transcendentals=0
        ),
        name="main_back",
    )(d_query, d_near, w_query, w_kv)


def finish_kernel(main_ref, low_ref, high_ref, states_ref, gain_ref, wkv_ref, out_ref):
    inner = low_ref.shape[2]
    d_keys = jnp.concatenate([low_ref[0], high_ref[0]], axis=0)
    d_values = jnp.concatenate([low_ref[1], high_ref[1]], axis=0)
    d_normed = main_ref[...] + dot_nt(d_keys, wkv_ref[:, :inner]) + dot_nt(d_values, wkv_ref[:, inner:])
    wide = states_ref[...].astype(F32)
    inv = inv_rms_of(wide)
    scaled = d_normed * gain_ref[...]
    mean = jnp.mean(scaled * wide, axis=-1, keepdims=True)
    out_ref[...] = (inv * scaled - wide * (inv * inv * inv * mean)).astype(BF)


def finish(main, low, high, states, gain, w_kv):
    toks, width = states.shape
    return pl.pallas_call(
        finish_kernel,
        out_shape=jax.ShapeDtypeStruct((toks, width), BF),
        compiler_params=pltpu.CompilerParams(vmem_limit_bytes=VMEM_LIMIT),
        cost_estimate=pl.CostEstimate(
            flops=4 * toks * width * low.shape[2], bytes_accessed=6 * toks * width, transcendentals=0
        ),
        name="finish",
    )(main, low, high, states, gain, w_kv)


def normed_of(states, gain):
    wide = states.astype(F32)
    return (wide * inv_rms_of(wide) * gain).astype(BF)


def halo_kernel(up_ref, down_ref, late_up_ref, late_down_ref, gain_ref, wkv_ref, out_ref):
    waits = lax.axis_index("seg") == lax.axis_size("seg") // 2
    up = jnp.where(waits, late_up_ref[...], up_ref[...])
    down = jnp.where(waits, late_down_ref[...], down_ref[...])
    normed = normed_of(jnp.concatenate([up, down], axis=0), gain_ref[...])
    out_ref[...] = dot(normed, wkv_ref[...]).astype(BF)


def project_halo(up, down, late_up, late_down, gain, w_kv):
    edge, width = up.shape
    double = w_kv.shape[1]
    return pl.pallas_call(
        halo_kernel,
        out_shape=jax.ShapeDtypeStruct((2 * edge, double), BF),
        compiler_params=pltpu.CompilerParams(vmem_limit_bytes=VMEM_LIMIT),
        cost_estimate=pl.CostEstimate(
            flops=4 * edge * width * double, bytes_accessed=4 * width * double, transcendentals=0
        ),
        name="project_halo",
    )(up, down, late_up, late_down, gain, w_kv)


def route():
    seg, band = lax.axis_index("seg"), lax.axis_index("lat")
    last = lax.axis_size("seg") // 2 - 1
    group = (band // 4) % 4
    relay_seg = jnp.where(group == 0, -1, 2 * group - 2)
    relays = seg == relay_seg
    sends = seg == jnp.where(group == 0, last, jnp.where(group == 1, -1, relay_seg - 1))
    late = (seg == last + 1) | (relays & (seg > 0))
    return relays, sends, late


def across_kernel(early_ref, own_ref, out_ref, held, sem):
    relays, sends, _ = route()

    def pass_on(source):
        copy_in = pltpu.make_async_copy(source, held, sem)
        copy_in.start()
        copy_in.wait()
        copy_out = pltpu.make_async_copy(held, out_ref, sem)
        copy_out.start()
        copy_out.wait()

    @pl.when(relays)
    def _():
        pass_on(early_ref)

    @pl.when(sends)
    def _():
        pass_on(own_ref)


def across_of(early, own):
    anywhere = pl.BlockSpec(memory_space=pl.ANY)
    return pl.pallas_call(
        across_kernel,
        in_specs=[anywhere, anywhere],
        out_specs=anywhere,
        out_shape=jax.ShapeDtypeStruct(own.shape, own.dtype),
        scratch_shapes=[pltpu.VMEM(own.shape, own.dtype), pltpu.SemaphoreType.DMA],
        name="across",
    )(early, own)


def edges_kernel(own_ref, up_ref, down_ref):
    edge = up_ref.shape[0]
    toks = own_ref.shape[0]
    up_ref[...] = own_ref[toks - edge :, :]
    down_ref[...] = own_ref[:edge, :]


def edges_of(own, edge):
    return pl.pallas_call(
        edges_kernel,
        out_shape=(jax.ShapeDtypeStruct((edge, own.shape[1]), own.dtype),) * 2,
        name="edges",
    )(own)


def memory_kernel(early_ref, late_ref, gain_ref, wkv_ref, out_ref, held, sem):
    _, _, late = route()

    @pl.when(late)
    def _():
        copy = pltpu.make_async_copy(late_ref, held, sem)
        copy.start()
        copy.wait()

    @pl.when(jnp.logical_not(late))
    def _():
        copy = pltpu.make_async_copy(early_ref, held, sem)
        copy.start()
        copy.wait()

    out_ref[...] = dot(normed_of(held[...], gain_ref[...]), wkv_ref[...]).astype(BF)


def project_memory(early, late, gain, w_kv):
    toks, width = early.shape
    double = w_kv.shape[1]
    vmem = pl.BlockSpec(memory_space=pltpu.VMEM)
    anywhere = pl.BlockSpec(memory_space=pl.ANY)
    return pl.pallas_call(
        memory_kernel,
        in_specs=[anywhere, anywhere, vmem, vmem],
        out_shape=jax.ShapeDtypeStruct((toks, double), BF),
        scratch_shapes=[pltpu.VMEM((toks, width), BF), pltpu.SemaphoreType.DMA],
        compiler_params=pltpu.CompilerParams(vmem_limit_bytes=VMEM_LIMIT),
        cost_estimate=pl.CostEstimate(
            flops=2 * toks * width * double, bytes_accessed=4 * width * double, transcendentals=0
        ),
        name="project_memory",
    )(early, late, gain, w_kv)


def shifted(value, axis, by):
    count = lax.axis_size(axis)
    pairs = [(i, i + by) for i in range(count) if 0 <= i + by < count]
    return lax.ppermute(value, axis, pairs)


def shifted_in(value, by, segs, bands, chosen):
    pairs = [
        (seg * bands + i, seg * bands + i + by)
        for seg in range(segs) if chosen(seg)
        for i in range(bands) if 0 <= i + by < bands
    ]
    return lax.ppermute(value, ("seg", "lat"), pairs)


def memory_routes(segs, bands):
    last = segs // 2 - 1
    relays = (last, 0, 2, 4)
    first, second = [], []
    for band in range(bands):
        relay = relays[(band // 4) % 4]
        for seg in range(segs - 1):
            pair = (seg * bands + band, (seg + 1) * bands + band)
            if seg == last:
                if relay != last:
                    first.append((pair[0], relay * bands + band))
                second.append((relay * bands + band, pair[1]))
            elif seg + 1 == relay and relay != last:
                second.append(pair)
            else:
                first.append(pair)
    return first, second


def body(states, norm_gain, w_query, w_kv, reach_rows, mem_keep, d_context):
    _, rows, lon, width = states.shape
    inner = w_query.shape[1]
    toks = rows * lon
    edge = HALO * lon
    flat = states.reshape(toks, width)
    gain = norm_gain.reshape(1, width)
    first, second = memory_routes(lax.axis_size("seg"), lax.axis_size("lat"))
    d_ctx = d_context.reshape(toks, inner)
    keep = mem_keep.reshape(1)
    segs, bands = lax.axis_size("seg"), lax.axis_size("lat")
    early, after = (lambda seg: seg != segs // 2), (lambda seg: seg == segs // 2)
    early_mem = lax.ppermute(flat, ("seg", "lat"), first)
    upper, lower = edges_of(flat, edge)
    up_states = shifted_in(upper, 1, segs, bands, early)
    down_states = shifted_in(lower, -1, segs, bands, early)
    across = across_of(early_mem, flat)
    across, own = lax.optimization_barrier((across, flat))
    late_mem = lax.ppermute(across, ("seg", "lat"), second)
    queries, keyval = project(own, gain, w_query, w_kv)
    up_states, down_states, upper, lower, queries, keyval = lax.optimization_barrier(
        (up_states, down_states, upper, lower, queries, keyval)
    )
    late_up = shifted_in(upper, 1, segs, bands, after)
    late_down = shifted_in(lower, -1, segs, bands, after)
    halo = project_halo(up_states, down_states, late_up, late_down, gain, w_kv)
    part, window, e_halo, d_halo = attend_window(reach_rows, keep, queries, keyval, halo, d_ctx)
    memory = project_memory(early_mem, late_mem, gain, w_kv)
    context, stats, g_halo, d_up, d_down = attend_outer(
        keep, queries, memory, d_ctx, part, window, e_halo, d_halo
    )
    high = shifted(d_up, "lat", -1)
    low = shifted(d_down, "lat", 1)
    d_query, d_near = attend_inner(
        reach_rows, keep, queries, keyval, halo, memory, d_ctx, stats, g_halo
    )
    main = main_back(d_query, d_near, w_query, w_kv)
    grad = finish(main, low, high, flat, gain, w_kv)
    return (
        context.reshape(1, rows, lon, inner),
        grad.reshape(1, rows, lon, width),
    )


def solution(mesh):
    tokens = P("seg", "lat", None, None)
    return jax.shard_map(
        body,
        mesh=mesh,
        in_specs=(tokens, P(), P(), P(), P("lat"), P("seg", "lat"), tokens),
        out_specs=(tokens, tokens),
        check_vma=False,
    )
```

time: 110 us -> 60.1 us (0.55)
  the two profiles are of different devices: /device:TPU:280 before, /device:TPU:448 now
where the time goes in v1:
time: 60.1 us; the launch traced here: 59.6 us
  Pallas kernels  22.2 us (37%)
  starting transfers between devices  21 us (35%)
  waiting for transfers between devices  11.7 us (19%)
  local copies, waits for them, and re-layouts  3.1 us (5%)
  between operations  1.59 us (3%)
    ppermute x4, waiting for transfers between devices, shifted_in(): return lax.ppermute(value, ('seg', 'lat'), pairs)  11.6 us
    ppermute x4, starting transfers between devices, shifted_in(): return lax.ppermute(value, ('seg', 'lat'), pairs)  9.43 us
    ppermute x2, starting transfers between devices, shifted(): return lax.ppermute(value, axis, pairs)  8.39 us
    pallas_call x1, Pallas kernels, attend_inner(): pl.pallas_call(inner_kernel, grid_spec=pltpu.PrefetchScalarGridSpec(num_s...  5.25 us
    pallas_call x1, Pallas kernels, attend_outer(): pl.pallas_call(outer_kernel, grid_spec=pltpu.PrefetchScalarGridSpec(num_s...  5.2 us
    pallas_call x1, Pallas kernels, attend_window(): pl.pallas_call(window_kernel, grid_spec=pltpu.PrefetchScalarGridSpec(num_...  4.35 us
    unnamed x24, local copies, waits for them, and re-layouts  3.1 us
    ppermute x1, starting transfers between devices, body(): early_mem = lax.ppermute(flat, ('seg', 'lat'), first)  1.91 us
  transfers between devices with their start and end apart: 8, of which 2 were waited for; matrix products, arithmetic and copies ran while one was open for 0% of the time, Pallas kernels for 24%

profile of v1, /device:TPU:448, one launch (start us, length us, event | category | flops | bytes accessed | tf_op | source)
XLA Modules:
  0.0 59.6 jit_solution(11990337743917843199)
XLA Ops:
  0.6 1.9 %collective-permute-start.2 = (bf16[256,1024]{1,0:T(8,128)(2,1)}, bf16[256,1024]{1,0:T(8,128)(2,1)S(1)}, u32[]{:S(2)}, u32[]{:S(2)}) collective-permute-start(bf16[256,1024]{1,0:T(8,128)(2,1)} %bitcast.9), channel_id=1, source_target_pairs={{0,32},{32,64},{64,96},{96,128},{128,160},{160,192},{192,224},{256... | collective-permute-start | bytes 1572872 | tf_op jit(solution)/shard_map/ppermute | solution.py:531
  2.6 1.8 %edges.1 = (bf16[128,1024]{1,0:T(8,128)(2,1)}, bf16[128,1024]{1,0:T(8,128)(2,1)}) custom-call(bf16[256,1024]{1,0:T(8,128)(2,1)} %bitcast.10), custom_call_target="tpu_custom_call" | custom-call | tf_op jit(solution)/shard_map/edges/pallas_call | solution.py:442
  4.4 0.7 %collective-permute-start = (bf16[128,1024]{1,0:T(8,128)(2,1)}, bf16[128,1024]{1,0:T(8,128)(2,1)S(1)}, u32[]{:S(2)}, u32[]{:S(2)}) collective-permute-start(bf16[128,1024]{1,0:T(8,128)(2,1)} %get-tuple-element.35), channel_id=1, source_target_pairs={{0,1},{1,2},{2,3},{3,4},{4,5},{5,6},{6,7},{7,8},{8,9},{9,10},{10,1... | collective-permute-start | bytes 786440 | tf_op jit(solution)/shard_map/ppermute | solution.py:497
  5.1 0.7 %collective-permute-start.1 = (bf16[128,1024]{1,0:T(8,128)(2,1)}, bf16[128,1024]{1,0:T(8,128)(2,1)S(1)}, u32[]{:S(2)}, u32[]{:S(2)}) collective-permute-start(bf16[128,1024]{1,0:T(8,128)(2,1)} %get-tuple-element.36), channel_id=1, source_target_pairs={{1,0},{2,1},{3,2},{4,3},{5,4},{6,5},{7,6},{8,7},{9,8},{10,9},{11,1... | collective-permute-start | bytes 786440 | tf_op jit(solution)/shard_map/ppermute | solution.py:497
  5.8 0.8 %copy-done.6 = bf16[256,1024]{1,0:T(8,128)(2,1)} copy-done((bf16[256,1024]{1,0:T(8,128)(2,1)}, bf16[256,1024]{1,0:T(8,128)(2,1)S(1)}, u32[]{:S(2)}) %copy-start.6) | copy-done | bytes 524312
  6.6 1.3 %collective-permute-start.3 = (bf16[256,1024]{1,0:T(8,128)(2,1)}, bf16[256,1024]{1,0:T(8,128)(2,1)S(1)}, u32[]{:S(2)}, u32[]{:S(2)}) collective-permute-start(bf16[256,1024]{1,0:T(8,128)(2,1)} %across.1), channel_id=1, source_target_pairs={{224,256},{225,257},{226,258},{227,259},{4,260},{5,261},{6,262},{7... | collective-permute-start | bytes 1572872 | tf_op jit(solution)/shard_map/ppermute | solution.py:537
  7.9 1.0 %copy-done.1 = bf16[1,8,32,1024]{3,2,1,0:T(8,128)(2,1)S(1)} copy-done((bf16[1,8,32,1024]{3,2,1,0:T(8,128)(2,1)S(1)}, bf16[1,8,32,1024]{3,2,1,0:T(8,128)(2,1)}, u32[]{:S(2)}) %copy-start.1) | copy-done | bytes 524312
  9.0 1.2 %copy-done.3 = bf16[1024,512]{1,0:T(8,128)(2,1)S(1)} copy-done((bf16[1024,512]{1,0:T(8,128)(2,1)S(1)}, bf16[1024,512]{1,0:T(8,128)(2,1)}, u32[]{:S(2)}) %copy-start.3) | copy-done | bytes 1048600
  10.2 1.1 %project.1 = (bf16[256,512]{1,0:T(8,128)(2,1)S(1)}, bf16[256,1024]{1,0:T(8,128)(2,1)S(1)}) custom-call(bf16[256,1024]{1,0:T(8,128)(2,1)S(1)} %bitcast.12, f32[1,1024]{1,0:T(1,128)S(1)} %bitcast.17, bf16[1024,512]{1,0:T(8,128)(2,1)S(1)} %copy-done.3, bf16[1024,1024]{1,0:T(8,128)(2,1)S(1)} %copy-done), custom_call_target="tpu_custom_call" | custom-call | flops 805306368 | bytes 3145728 | tf_op jit(solution)/shard_map/project/pallas_call | solution.py:39
  11.3 0.0 copy-start.5
  11.3 3.6 %collective-permute-start.4 = (bf16[128,1024]{1,0:T(8,128)(2,1)S(1)}, bf16[128,1024]{1,0:T(8,128)(2,1)S(1)}, u32[]{:S(2)}, u32[]{:S(2)}) collective-permute-start(bf16[128,1024]{1,0:T(8,128)(2,1)S(1)} %copy-done.11), channel_id=1, source_target_pairs={{256,257},{257,258},{258,259},{259,260},{260,261},{261,262},{262,2... | collective-permute-start | bytes 786440 | tf_op jit(solution)/shard_map/ppermute | solution.py:497
  15.0 4.5 %collective-permute-start.5 = (bf16[128,1024]{1,0:T(8,128)(2,1)S(1)}, bf16[128,1024]{1,0:T(8,128)(2,1)S(1)}, u32[]{:S(2)}, u32[]{:S(2)}) collective-permute-start(bf16[128,1024]{1,0:T(8,128)(2,1)S(1)} %copy-done.10), channel_id=1, source_target_pairs={{257,256},{258,257},{259,258},{260,259},{261,260},{262,261},{263,2... | collective-permute-start | bytes 786440 | tf_op jit(solution)/shard_map/ppermute | solution.py:497
  20.1 1.8 %collective-permute-done.4.late_up_ref = bf16[128,1024]{1,0:T(8,128)(2,1)S(1)} collective-permute-done((bf16[128,1024]{1,0:T(8,128)(2,1)S(1)}, bf16[128,1024]{1,0:T(8,128)(2,1)S(1)}, u32[]{:S(2)}, u32[]{:S(2)}) %collective-permute-start.4) | collective-permute-done | bytes 262176 | tf_op jit(solution)/shard_map/ppermute | solution.py:497
  21.8 9.9 %collective-permute-done.5.late_down_ref = bf16[128,1024]{1,0:T(8,128)(2,1)S(1)} collective-permute-done((bf16[128,1024]{1,0:T(8,128)(2,1)S(1)}, bf16[128,1024]{1,0:T(8,128)(2,1)S(1)}, u32[]{:S(2)}, u32[]{:S(2)}) %collective-permute-start.5) | collective-permute-done | bytes 262176 | tf_op jit(solution)/shard_map/ppermute | solution.py:497
  31.7 0.9 %project_halo.1.ku_ref.vu_ref.kd_ref.vd_ref = bf16[256,1024]{1,0:T(8,128)(2,1)S(1)} custom-call(bf16[128,1024]{1,0:T(8,128)(2,1)S(1)} %collective-permute-done.up_ref, bf16[128,1024]{1,0:T(8,128)(2,1)S(1)} %collective-permute-done.1.down_ref, bf16[128,1024]{1,0:T(8,128)(2,1)S(1)} %collective-permute-done.4.late_up_ref, ...), custom_call_target="tpu_custom_call" | custom-call | flops 536870912 | bytes 4194304 | tf_op jit(solution)/shard_map/project_halo/pallas_call | solution.py:380
  32.6 4.3 %attend_window.1 = (f32[512,256]{1,0:T(8,128)S(1)}, f32[4,8,256]{2,1,0:T(8,128)S(1)}, f32[8,128,256]{2,1,0:T(8,128)S(1)}, f32[8,128,256]{2,1,0:T(8,128)S(1)}) custom-call(s32[8]{0:T(128)S(1)} %copy-done.9, s32[1]{0:T(128)} %bitcast.6.keep_ref, bf16[256,512]{1,0:T(8,128)(2,1)S(1)} %get-tuple-element.30.q_ref, ...), custom_call_target="tpu_custom_call" | custom-call | flops 805306368 | bytes 5242880 | tf_op jit(solution)/shard_map/attend_window/pallas_call | solution.py:226
  37.0 0.9 %project_memory.1.km_ref.vm_ref = bf16[256,1024]{1,0:T(8,128)(2,1)S(1)} custom-call(bf16[256,1024]{1,0:T(8,128)(2,1)S(1)} %copy-done.7, bf16[256,1024]{1,0:T(8,128)(2,1)S(1)} %collective-permute-done.3.late_ref, f32[1,1024]{1,0:T(1,128)S(1)} %bitcast.19, bf16[1024,1024]{1,0:T(8,128)(2,1)S(1)} %copy-done), custom_call_target="tpu_custom_call" | custom-call | flops 536870912 | bytes 4194304 | tf_op jit(solution)/shard_map/project_memory/pallas_call | solution.py:472
  37.9 5.2 %attend_outer.1 = (bf16[256,512]{1,0:T(8,128)(2,1)}, f32[4,8,256]{2,1,0:T(8,128)S(1)}, bf16[8,128,256]{2,1,0:T(8,128)(2,1)S(1)}, bf16[2,128,512]{2,1,0:T(8,128)(2,1)S(1)}, bf16[2,128,512]{2,1,0:T(8,128)(2,1)S(1)}) custom-call(s32[1]{0:T(128)} %bitcast.7.keep_ref, bf16[256,512]{1,0:T(8,128)(2,1)S(1)} %get-tuple-element.30.q_ref, ...), custom_call_target="tpu_custom_call" | custom-call | flops 402653184 | bytes 5242880 | tf_op jit(solution)/shard_map/attend_outer/pallas_call | solution.py:258
  43.1 1.9 %collective-permute-start.6 = (bf16[2,128,512]{2,1,0:T(8,128)(2,1)S(1)}, bf16[2,128,512]{2,1,0:T(8,128)(2,1)S(1)}, u32[]{:S(2)}, u32[]{:S(2)}) collective-permute-start(bf16[2,128,512]{2,1,0:T(8,128)(2,1)S(1)} %get-tuple-element.46), channel_id=1, source_target_pairs={{0,1},{1,2},{2,3},{3,4},{4,5},{5,6},{6,7},{7,8},{8,9},{9,10},{10,1... | collective-permute-start | bytes 786440 | tf_op jit(solution)/shard_map/ppermute | solution.py:488
  45.0 6.5 %collective-permute-start.7 = (bf16[2,128,512]{2,1,0:T(8,128)(2,1)S(1)}, bf16[2,128,512]{2,1,0:T(8,128)(2,1)S(1)}, u32[]{:S(2)}, u32[]{:S(2)}) collective-permute-start(bf16[2,128,512]{2,1,0:T(8,128)(2,1)S(1)} %get-tuple-element.47), channel_id=1, source_target_pairs={{1,0},{2,1},{3,2},{4,3},{5,4},{6,5},{7,6},{8,7},{9,8},{10,9},{11,1... | collective-permute-start | bytes 786440 | tf_op jit(solution)/shard_map/ppermute | solution.py:488
  51.5 0.0 copy-start.4
  51.5 5.3 %attend_inner.1 = (bf16[256,512]{1,0:T(8,128)(2,1)S(1)}, bf16[2,256,512]{2,1,0:T(8,128)(2,1)S(1)}) custom-call(s32[8]{0:T(128)S(1)} %copy-done.9, s32[1]{0:T(128)} %bitcast.8.keep_ref, bf16[256,512]{1,0:T(8,128)(2,1)S(1)} %get-tuple-element.30.q_ref, bf16[256,1024]{1,0:T(8,128)(2,1)S(1)} %get-tuple-element.32.k_ref.v_ref, ...), custom_call_target="tpu_custom_call" | custom-call | flops 805306368 | bytes 5242880 | tf_op jit(solution)/shard_map/attend_inner/pallas_call | solution.py:293
  56.8 1.0 %main_back.1.main_ref = f32[256,1024]{1,0:T(8,128)S(1)} custom-call(bf16[256,512]{1,0:T(8,128)(2,1)S(1)} %get-tuple-element.44.dq_ref, bf16[2,256,512]{2,1,0:T(8,128)(2,1)S(1)} %get-tuple-element.45.dnear_ref, bf16[1024,512]{1,0:T(8,128)(2,1)S(1)} %copy-done.4, bf16[1024,1024]{1,0:T(8,128)(2,1)S(1)} %copy-done), custom_call_target="tpu_custom_call" | custom-call | flops 805306368 | bytes 3145728 | tf_op jit(solution)/shard_map/main_back/pallas_call | solution.py:328
  57.8 1.7 %finish.1 = bf16[256,1024]{1,0:T(8,128)(2,1)} custom-call(f32[256,1024]{1,0:T(8,128)S(1)} %main_back.1.main_ref, bf16[2,128,512]{2,1,0:T(8,128)(2,1)S(1)} %collective-permute-done.6.low_ref, bf16[2,128,512]{2,1,0:T(8,128)(2,1)S(1)} %collective-permute-done.7.high_ref, bf16[256,1024]{1,0:T(8,128)(2,1)S(1)} %bitcast.13, f32[1,1024]{1,0:T(1,128)S(1)} %bitcast.20, ...), custom_call_target="tpu_custom_call" | custom-call | flops 536870912 | bytes 1572864 | tf_op jit(solution)/shard_map/finish/pallas_call | solution.py:353
  (26 shorter events, 0.1 us)
Async XLA Ops:
  0.6 7.3 %copy-start = (bf16[1024,1024]{1,0:T(8,128)(2,1)S(1)}, bf16[1024,1024]{1,0:T(8,128)(2,1)}, u32[]{:S(2)}) copy-start(bf16[1024,1024]{1,0:T(8,128)(2,1)} %wkv_ref.9) | copy-start | bytes 6291460
  0.6 7.3 %copy-start.8 = (f32[1024]{0:T(1024)S(1)}, f32[1024]{0:T(1024)}, u32[]{:S(2)}) copy-start(f32[1024]{0:T(1024)} %param.8) | copy-start | bytes 12292
  0.6 5.1 %collective-permute-start.2 = (bf16[256,1024]{1,0:T(8,128)(2,1)}, bf16[256,1024]{1,0:T(8,128)(2,1)S(1)}, u32[]{:S(2)}, u32[]{:S(2)}) collective-permute-start(bf16[256,1024]{1,0:T(8,128)(2,1)} %bitcast.9), channel_id=1, source_target_pairs={{0,32},{32,64},{64,96},{96,128},{128,160},{160,192},{192,224},{256... | collective-permute-start | bytes 1572872 | tf_op jit(solution)/shard_map/ppermute | solution.py:531
  4.4 6.9 %collective-permute-start = (bf16[128,1024]{1,0:T(8,128)(2,1)}, bf16[128,1024]{1,0:T(8,128)(2,1)S(1)}, u32[]{:S(2)}, u32[]{:S(2)}) collective-permute-start(bf16[128,1024]{1,0:T(8,128)(2,1)} %get-tuple-element.35), channel_id=1, source_target_pairs={{0,1},{1,2},{2,3},{3,4},{4,5},{5,6},{6,7},{7,8},{8,9},{9,10},{10,1... | collective-permute-start | bytes 786440 | tf_op jit(solution)/shard_map/ppermute | solution.py:497
  5.1 6.2 %collective-permute-start.1 = (bf16[128,1024]{1,0:T(8,128)(2,1)}, bf16[128,1024]{1,0:T(8,128)(2,1)S(1)}, u32[]{:S(2)}, u32[]{:S(2)}) collective-permute-start(bf16[128,1024]{1,0:T(8,128)(2,1)} %get-tuple-element.36), channel_id=1, source_target_pairs={{1,0},{2,1},{3,2},{4,3},{5,4},{6,5},{7,6},{8,7},{9,8},{10,9},{11,1... | collective-permute-start | bytes 786440 | tf_op jit(solution)/shard_map/ppermute | solution.py:497
  5.8 0.8 %copy-start.6 = (bf16[256,1024]{1,0:T(8,128)(2,1)}, bf16[256,1024]{1,0:T(8,128)(2,1)S(1)}, u32[]{:S(2)}) copy-start(bf16[256,1024]{1,0:T(8,128)(2,1)S(1)} %collective-permute-done.2.early_ref) | copy-start | bytes 1572868
  6.6 30.4 %collective-permute-start.3 = (bf16[256,1024]{1,0:T(8,128)(2,1)}, bf16[256,1024]{1,0:T(8,128)(2,1)S(1)}, u32[]{:S(2)}, u32[]{:S(2)}) collective-permute-start(bf16[256,1024]{1,0:T(8,128)(2,1)} %across.1), channel_id=1, source_target_pairs={{224,256},{225,257},{226,258},{227,259},{4,260},{5,261},{6,262},{7... | collective-permute-start | bytes 1572872 | tf_op jit(solution)/shard_map/ppermute | solution.py:537
  7.9 1.0 %copy-start.1 = (bf16[1,8,32,1024]{3,2,1,0:T(8,128)(2,1)S(1)}, bf16[1,8,32,1024]{3,2,1,0:T(8,128)(2,1)}, u32[]{:S(2)}) copy-start(bf16[1,8,32,1024]{3,2,1,0:T(8,128)(2,1)} %param.7) | copy-start | bytes 1572868
  9.0 1.2 %copy-start.3 = (bf16[1024,512]{1,0:T(8,128)(2,1)S(1)}, bf16[1024,512]{1,0:T(8,128)(2,1)}, u32[]{:S(2)}) copy-start(bf16[1024,512]{1,0:T(8,128)(2,1)} %wq_ref.3) | copy-start | bytes 3145732
  10.2 1.1 %copy-start.11 = (bf16[128,1024]{1,0:T(8,128)(2,1)S(1)}, bf16[128,1024]{1,0:T(8,128)(2,1)}, u32[]{:S(2)}) copy-start(bf16[128,1024]{1,0:T(8,128)(2,1)} %get-tuple-element.35) | copy-start | bytes 786436
  10.2 4.8 %copy-start.10 = (bf16[128,1024]{1,0:T(8,128)(2,1)S(1)}, bf16[128,1024]{1,0:T(8,128)(2,1)}, u32[]{:S(2)}) copy-start(bf16[128,1024]{1,0:T(8,128)(2,1)} %get-tuple-element.36) | copy-start | bytes 786436
  11.3 21.3 %copy-start.5 = (bf16[1,8,32,512]{3,2,1,0:T(8,128)(2,1)S(1)}, bf16[1,8,32,512]{3,2,1,0:T(8,128)(2,1)}, u32[]{:S(2)}) copy-start(bf16[1,8,32,512]{3,2,1,0:T(8,128)(2,1)} %param.13) | copy-start | bytes 786436
  11.3 21.3 %copy-start.9 = (s32[8]{0:T(128)S(1)}, s32[8]{0:T(128)}, u32[]{:S(2)}) copy-start(s32[8]{0:T(128)} %reach_ref.3) | copy-start | bytes 100
  11.3 10.5 %collective-permute-start.4 = (bf16[128,1024]{1,0:T(8,128)(2,1)S(1)}, bf16[128,1024]{1,0:T(8,128)(2,1)S(1)}, u32[]{:S(2)}, u32[]{:S(2)}) collective-permute-start(bf16[128,1024]{1,0:T(8,128)(2,1)S(1)} %copy-done.11), channel_id=1, source_target_pairs={{256,257},{257,258},{258,259},{259,260},{260,261},{261,262},{262,2... | collective-permute-start | bytes 786440 | tf_op jit(solution)/shard_map/ppermute | solution.py:497
  15.0 16.8 %collective-permute-start.5 = (bf16[128,1024]{1,0:T(8,128)(2,1)S(1)}, bf16[128,1024]{1,0:T(8,128)(2,1)S(1)}, u32[]{:S(2)}, u32[]{:S(2)}) collective-permute-start(bf16[128,1024]{1,0:T(8,128)(2,1)S(1)} %copy-done.10), channel_id=1, source_target_pairs={{257,256},{258,257},{259,258},{260,259},{261,260},{262,261},{263,2... | collective-permute-start | bytes 786440 | tf_op jit(solution)/shard_map/ppermute | solution.py:497
  32.6 4.4 %copy-start.7 = (bf16[256,1024]{1,0:T(8,128)(2,1)S(1)}, bf16[256,1024]{1,0:T(8,128)(2,1)}, u32[]{:S(2)}) copy-start(bf16[256,1024]{1,0:T(8,128)(2,1)} %copy-done.6) | copy-start | bytes 1572868
  43.1 14.7 %collective-permute-start.6 = (bf16[2,128,512]{2,1,0:T(8,128)(2,1)S(1)}, bf16[2,128,512]{2,1,0:T(8,128)(2,1)S(1)}, u32[]{:S(2)}, u32[]{:S(2)}) collective-permute-start(bf16[2,128,512]{2,1,0:T(8,128)(2,1)S(1)} %get-tuple-element.46), channel_id=1, source_target_pairs={{0,1},{1,2},{2,3},{3,4},{4,5},{5,6},{6,7},{7,8},{8,9},{9,10},{10,1... | collective-permute-start | bytes 786440 | tf_op jit(solution)/shard_map/ppermute | solution.py:488
  45.0 12.8 %collective-permute-start.7 = (bf16[2,128,512]{2,1,0:T(8,128)(2,1)S(1)}, bf16[2,128,512]{2,1,0:T(8,128)(2,1)S(1)}, u32[]{:S(2)}, u32[]{:S(2)}) collective-permute-start(bf16[2,128,512]{2,1,0:T(8,128)(2,1)S(1)} %get-tuple-element.47), channel_id=1, source_target_pairs={{1,0},{2,1},{3,2},{4,3},{5,4},{6,5},{7,6},{8,7},{9,8},{10,9},{11,1... | collective-permute-start | bytes 786440 | tf_op jit(solution)/shard_map/ppermute | solution.py:488
  51.5 5.3 %copy-start.4 = (bf16[1024,512]{1,0:T(8,128)(2,1)S(1)}, bf16[1024,512]{1,0:T(8,128)(2,1)}, u32[]{:S(2)}) copy-start(bf16[1024,512]{1,0:T(8,128)(2,1)} %wq_ref.3) | copy-start | bytes 3145732
  56.8 1.1 %copy-start.2 = (bf16[1,8,32,1024]{3,2,1,0:T(8,128)(2,1)S(1)}, bf16[1,8,32,1024]{3,2,1,0:T(8,128)(2,1)}, u32[]{:S(2)}) copy-start(bf16[1,8,32,1024]{3,2,1,0:T(8,128)(2,1)} %param.7) | copy-start | bytes 1572868
